TPU v7x, 32 devices: a whole 2x2x4 slice. The times are simulated.
32 devices in a mesh: ctx: 8 (over y, x, core), tp: 4 (over z).
Axes of the slice: x: 2, y: 2, z: 4, core: 2. Of those that a mesh axis runs over, the one named last changes fastest.
Arguments:
- queries: bfloat16 [2048, 8192], P('ctx', 'tp'), may hold values from -100 to 100
- key_rows: bfloat16 [2048, 1024], P('ctx'), may hold values from -5 to 5
- value_rows: bfloat16 [2048, 1024], P('ctx'), may hold values from -6 to 6
- documents: int32 [2048], P('ctx'), may hold values from 0 to 3, never falling along the last dimension, each value on 1 to 1536 neighbouring positions
- out_weight: bfloat16 [8192, 8192], P('tp', 'ctx'), may hold values from -0.75 to 0.75
Outputs:
- attention_out: bfloat16 [2048, 8192], P(('ctx', 'tp'))
Inputs may be any that keep to these rules, and one draw needn't show every extreme that they name: `documents`: document numbers never fall along the window; each document holds 1 to 1536 tokens and one holds exactly 1536.
All inputs are finite; a program needn't handle non-finite values.
Results may differ from a plain program's by a relative error of at most 0.015.
Values may be sent and summed in bfloat16 or wider, within the bound.
A program may use at most 128 MiB of HBM per device.

v0:
```python
import math

import jax
import jax.numpy as jnp
from jax import lax
from jax.sharding import PartitionSpec as P

HEADS = 64
KV_HEADS = 8
HD = 128


def absorb_group(state, query_block, query_pos, query_docs, piece, start):
    piece_keys, piece_values, piece_docs = piece
    length = piece_keys.shape[0]
    kv_here = query_block.shape[1]
    scale = 1.0 / math.sqrt(HD)

    def update(inner):
        old_max, old_sum, old_acc = inner
        key_block = piece_keys.reshape(length, kv_here, HD)
        value_block = piece_values.reshape(length, kv_here, HD)
        scores = (
            jnp.einsum("tghd,ngd->ghtn", query_block, key_block, preferred_element_type=jnp.float32)
            * scale
        )
        key_pos = jnp.arange(length, dtype=jnp.int32)
        allowed = (key_pos[None, :] <= query_pos[:, None]) & (
            piece_docs[None, :] == query_docs[:, None]
        )
        new_max = jnp.maximum(old_max, jnp.max(jnp.where(allowed, scores, -1e30), axis=3))
        weights = jnp.where(allowed, jnp.exp(scores - new_max[..., None]), 0.0)
        new_sum = jnp.sum(weights, axis=3)
        weighted = jnp.einsum(
            "ghtn,ngd->tghd",
            weights.astype(jnp.bfloat16),
            value_block,
            preferred_element_type=jnp.float32,
        )
        return (new_max, new_sum, weighted)

    return lax.cond(start <= query_pos[-1], update, lambda inner: inner, state)


def empty_state(rows, kv_here, per_kv):
    return (
        jnp.full((kv_here, per_kv, rows), -1e30, jnp.float32),
        jnp.zeros((kv_here, per_kv, rows), jnp.float32),
        jnp.zeros((rows, kv_here, per_kv, HD), jnp.float32),
    )


def finish(state):
    run_max, run_sum, run_acc = state
    rows = run_acc.shape[0]
    attended = (run_acc / jnp.transpose(run_sum, (2, 0, 1))[..., None]).astype(jnp.bfloat16)
    return attended.reshape(rows, run_acc.shape[1] * run_acc.shape[2] * HD)


def on_device(queries, key_rows, value_rows, documents, out_weight):
    tokens_here = queries.shape[0]
    heads_here = queries.shape[1] // HD
    group_size = HEADS // KV_HEADS
    kv_here = max(1, heads_here // group_size)
    per_kv = heads_here // kv_here
    kv_first = lax.axis_index("tp") * heads_here // group_size
    own_keys = lax.dynamic_slice_in_dim(key_rows, kv_first * HD, kv_here * HD, 1)
    own_values = lax.dynamic_slice_in_dim(value_rows, kv_first * HD, kv_here * HD, 1)
    query_blocks = queries.reshape(tokens_here, kv_here, per_kv, HD)
    first_row = lax.axis_index("ctx") * tokens_here
    groups = [(query_blocks, first_row + jnp.arange(tokens_here, dtype=jnp.int32), documents)]
    initial = tuple((empty_state(group[0].shape[0], kv_here, per_kv) for group in groups))
    piece = (
        lax.all_gather(own_keys, "ctx", axis=0, tiled=True),
        lax.all_gather(own_values, "ctx", axis=0, tiled=True),
        lax.all_gather(documents, "ctx", axis=0, tiled=True),
    )
    start = jnp.int32(0)
    states = tuple(
        (
            absorb_group(
                initial[index], groups[index][0], groups[index][1], groups[index][2], piece, start
            )
            for index in range(len(groups))
        )
    )
    attended = finish(states[0])
    terms = jnp.dot(
        attended,
        lax.all_gather(out_weight, "ctx", axis=1, tiled=True),
        preferred_element_type=jnp.float32,
    )
    summed = lax.psum_scatter(terms.astype(jnp.bfloat16), "tp", scatter_dimension=0, tiled=True)
    return summed


def solution(mesh):
    in_specs = (P("ctx", "tp"), P("ctx", None), P("ctx", None), P("ctx"), P("tp", "ctx"))
    out_specs = P(("ctx", "tp"), None)
    return jax.shard_map(
        on_device, mesh=mesh, in_specs=in_specs, out_specs=out_specs, check_vma=False
    )
```

profile of v0, /device:TPU:9, one launch (start us, length us, event | category | flops | bytes accessed | tf_op | source)
XLA Modules:
  0.0 322.4 jit_solution(12014025802697955196)
XLA Ops:
  6.5 0.0 copy-start
  6.5 0.0 all-gather.5.cloned.1.call-start
  6.5 1.0 copy-done
  7.6 0.7 constant_dynamic-slice_fusion.1
  8.2 0.0 all-gather.5.cloned.1.call-update
  8.3 0.0 all-gather.7.cloned.1.call-start
  8.3 1.6 constant_dynamic-slice_fusion
  9.9 0.0 all-gather.7.cloned.1.call-update
  9.9 0.0 all-gather.9.cloned.1.call-start
  10.0 0.7 all-gather.9.cloned.1.call-update
  10.7 0.0 reduce-scatter.2.cloned.1.call-start
  10.7 0.6 slice.3
  12.0 9.5 %all-gather = s32[8,1,256]{2,1,0:T(1,128)S(1)} all-gather(s32[1,1,256]{2,1,0:T(1,128)} %bitcast.37), channel_id=1, replica_groups=mesh['ctx'=8,'tp'=4] {'ctx'}, dimensions={0}, use_global_device_ids=true | all-gather | bytes 9216 | tf_op jit(solution)/shard_map/all_gather | solution.py:76
  21.5 12.9 %all-gather.5.cloned.1.call-done = bf16[2048,256]{1,0:T(8,128)(2,1)} async-done(((bf16[256,256]{1,0:T(8,128)(2,1)}), bf16[2048,256]{1,0:T(8,128)(2,1)}) %all-gather.5.cloned.1.call-update) | async-done | bytes 1048592 | tf_op jit(solution)/shard_map/all_gather | solution.py:74
  34.4 25.4 %all-gather.7.cloned.1.call-done = bf16[2048,256]{1,0:T(8,128)(2,1)} async-done(((bf16[256,256]{1,0:T(8,128)(2,1)}), bf16[2048,256]{1,0:T(8,128)(2,1)}) %all-gather.7.cloned.1.call-update) | async-done | bytes 1048592 | tf_op jit(solution)/shard_map/all_gather | solution.py:75
  59.8 56.6 %conditional.1 = (f32[2,8,256]{2,1,0:T(8,128)S(1)}, f32[256,2,8,128]{0,3,2,1:T(8,128)S(1)}) conditional(s32[]{:T(128)} %bitcast.4, () %tuple.13, (s32[256]{0:T(256)S(1)}, s32[2048]{0:T(1024)S(1)}, s32[256]{0:T(256)}, bf16[2048,256]{1,0:T(8,128)(2,1)}, bf16[256,2048]{1,0:T(8,128)(2,1)}, /*index=5*/bf16[2048,256]{1,0:T(8,128)(2,1)}) %tuple.28), branch_computations={%region_0.1_spmd, %region_1.4_spmd} | conditional | flops 4388810752 | bytes 122791976 | solution.py:42
  59.8 1.3 fusion.8
  61.1 1.5 copy.30
  62.5 2.1 reshape.20
  64.6 0.0 copy-start.2
  64.7 18.2 %fusion = (f32[2,8,256]{2,1,0:T(8,128)S(1)}, f32[2,2048,256,8]{2,1,3,0:T(8,128)}) fusion(pred[256,2048]{0,1:T(8,128)(4,1)S(1)} %fusion.8, bf16[256,2,8,128]{3,2,1,0:T(8,128)(2,1)S(1)} %bitcast.32, bf16[2048,2,128,1]{2,1,0,3:T(2,128)(2,1)} %bitcast.33), kind=kOutput, calls=%fused_computation.2 | convolution fusion | flops 2172645376 | bytes 36192256 | tf_op jit(solution)/shard_map/cond/branch_1_fun/tghd,ngd->ghtn/dot_general | solution.py:24
  82.9 14.4 %fusion.4 = f32[2,8,256]{2,1,0:T(8,128)S(1)} fusion(f32[2,2048,256,8]{2,1,3,0:T(8,128)} %get-tuple-element.32, f32[2,8,256]{2,1,0:T(8,128)S(1)} %broadcast_maximum_fusion, pred[256,2048]{0,1:T(8,128)(4,1)S(1)} %fusion.8), kind=kLoop, calls=%fused_computation.6 | loop fusion | flops 33550336 | bytes 34111488 | tf_op jit(solution)/shard_map/cond/branch_1_fun/reduce_sum | solution.py:33
  97.3 0.0 copy-done.2
  97.3 0.3 reshape.22
  97.6 16.7 %fusion.9 = f32[256,2,8,128]{3,0,2,1:T(8,128)} fusion(f32[2,2048,256,8]{2,1,3,0:T(8,128)} %get-tuple-element.32, f32[2,8,256]{2,1,0:T(8,128)S(1)} %broadcast_maximum_fusion, pred[256,2048]{0,1:T(8,128)(4,1)S(1)} %fusion.8, bf16[2048,2,128,1]{2,1,0,3:T(2,128)(2,1)S(1)} %bitcast.34), kind=kOutput, calls=%fused_computation.11 | convolution fusion | flops 2181038080 | bytes 37240832 | tf_op jit(solution)/shard_map/cond/branch_1_fun/ghtn,ngd->tghd/dot_general | solution.py:34
  114.2 1.9 copy.29
  116.3 0.0 copy-start.1
  116.4 1.2 divide_convert_fusion
  117.5 105.0 %all-gather.9.cloned.1.call-done = bf16[2048,8192]{1,0:T(8,128)(2,1)} async-done(((bf16[2048,1024]{1,0:T(8,128)(2,1)}), bf16[2048,8192]{1,0:T(8,128)(2,1)}) %all-gather.9.cloned.1.call-update) | async-done | bytes 33554448 | tf_op jit(solution)/shard_map/all_gather | solution.py:90
  222.5 16.8 %convolution_convert_fusion = bf16[256,8192]{1,0:T(8,128)(2,1)} fusion(bf16[256,2048]{0,1:T(8,128)(2,1)} %bitcast.30, bf16[2048,8192]{1,0:T(8,128)(2,1)} %all-gather.9.cloned.1.call-done), kind=kOutput, calls=%fused_computation.19 | convolution fusion | flops 8592031744 | bytes 38797312 | tf_op jit(solution)/shard_map/dot_general | solution.py:88
  239.3 0.0 reduce-scatter.2.cloned.1.call-update
  239.3 76.6 %reduce-scatter.2.cloned.1.call-done = bf16[64,8192]{1,0:T(8,128)(2,1)} async-done(((bf16[256,8192]{1,0:T(8,128)(2,1)}), bf16[64,8192]{1,0:T(8,128)(2,1)}) %reduce-scatter.2.cloned.1.call-update) | async-done | bytes 1048592 | tf_op jit(solution)/shard_map/reduce_scatter | solution.py:93
  315.9 0.0 copy-done.1
  (2 shorter events, 0.0 us)
Async XLA Ops:
  6.5 1.0 copy-start
  6.5 27.8 %all-gather.5.cloned.1.call-start = ((), (), s32[]{:S(2)}) async-start(), calls=%async_computation.1 | async-start | bytes 1179648 | tf_op jit(solution)/shard_map/all_gather | solution.py:74
  8.3 51.5 %all-gather.7.cloned.1.call-start = ((), (), s32[]{:S(2)}) async-start(), calls=%async_computation.2 | async-start | bytes 1179648 | tf_op jit(solution)/shard_map/all_gather | solution.py:75
  9.9 212.6 %all-gather.9.cloned.1.call-start = ((), (), s32[]{:S(2)}) async-start(), calls=%async_computation.3 | async-start | bytes 37748736 | tf_op jit(solution)/shard_map/all_gather | solution.py:90
  10.7 305.2 %reduce-scatter.2.cloned.1.call-start = ((), (), s32[]{:S(2)}) async-start(), calls=%async_computation.4 | async-start | bytes 5242880 | tf_op jit(solution)/shard_map/reduce_scatter | solution.py:93
  64.6 32.6 %copy-start.2 = (bf16[2048,256]{1,0:T(8,128)(2,1)S(1)}, bf16[2048,256]{1,0:T(8,128)(2,1)}, u32[]{:S(2)}) copy-start(bf16[2048,256]{1,0:T(8,128)(2,1)} %get-tuple-element.23) | copy-start | bytes 3145732 | tf_op jit(solution)/shard_map/cond
  116.3 199.5 %copy-start.1 = (bf16[256,1024]{1,0:T(8,128)(2,1)S(1)}, bf16[256,1024]{1,0:T(8,128)(2,1)}, u32[]{:S(2)}) copy-start(bf16[256,1024]{1,0:T(8,128)(2,1)} %param.8) | copy-start | bytes 1572868
Sparse Core Ops, SparseCore 0:
  9.2 25.0 all-gather.4
  36.3 23.4 all-gather.6
  61.7 160.7 all-gather.8
  239.4 76.3 reduce-scatter.1
where the time goes:
time: 324 us; the launch traced here: 322 us
  waiting for transfers between devices  221 us (68%)
  matrix products  51.7 us (16%)
  other arithmetic  16.8 us (5%)
  between operations  13.8 us (4%)
  local copies, waits for them, and re-layouts  9.73 us (3%)
  blocking collectives  9.52 us (3%)
    all_gather x1, waiting for transfers between devices, on_device(): lax.all_gather(out_weight, 'ctx', axis=1, tiled=True)  105 us
    reduce_scatter x1, waiting for transfers between devices, on_device(): lax.psum_scatter(terms.astype(jnp.bfloat16), 'tp', scatter_dimension=0, t...  76.6 us
    all_gather x1, waiting for transfers between devices, on_device(): lax.all_gather(own_values, 'ctx', axis=0, tiled=True)  25.4 us
    dot_general x1, matrix products, update(): jnp.einsum('tghd,ngd->ghtn', query_block, key_block, preferred_element_ty...  18.2 us
    dot_general x1, matrix products, on_device(): jnp.dot(attended, lax.all_gather(out_weight, 'ctx', axis=1, tiled=True),...  16.8 us
    dot_general x1, matrix products, update(): jnp.einsum('ghtn,ngd->tghd', weights.astype(jnp.bfloat16), value_block, p...  16.7 us
    reduce_sum x1, other arithmetic, update(): new_sum = jnp.sum(weights, axis=3)  14.4 us
    all_gather x1, waiting for transfers between devices, on_device(): lax.all_gather(own_keys, 'ctx', axis=0, tiled=True)  12.9 us
  transfers between devices with their start and end apart: 4, of which 4 were waited for; matrix products, arithmetic and copies ran while one was open for 19% of the time, Pallas kernels for 0%

commit v1 on v0

v1 whole, which is shorter than its diff:
```python
import functools
import math

import jax
import jax.numpy as jnp
from jax import lax
from jax.experimental import pallas as pl
from jax.experimental.pallas import tpu as pltpu
from jax.sharding import PartitionSpec as P

HEADS = 64
KV_HEADS = 8
HD = 128
MESH = pl.DeviceIdType.MESH
F32 = jnp.float32
BF16 = jnp.bfloat16
SCALE2 = math.log2(math.e) / math.sqrt(HD)
UNITS = 4


def fused_kernel(
    q_ref, k_ref, v_ref, dcol_ref, drow_ref, w_hbm, out_ref,
    w_ref, kv, docs, att, part, zin, fin,
    w_sem, kv_send, kv_recv, doc_send, doc_recv,
    att_send, att_recv, z_send, z_recv, x_send, x_recv,
):
    c = lax.axis_index("ctx")
    z = lax.axis_index("tp")
    ctx = kv.shape[0]
    tokens = q_ref.shape[0]
    rows = att.shape[2]
    kv_here = kv.shape[2] // (2 * HD)
    per_kv = q_ref.shape[1] // HD // kv_here
    unit = part.shape[3]
    width = UNITS * unit

    y, x, core = c // 4, (c // 2) % 2, c % 2

    def at(yy, xx, cc):
        return yy * 4 + xx * 2 + cc

    sib, xn, yn = at(y, x, 1 - core), at(y, 1 - x, core), at(1 - y, x, core)
    dg = at(1 - y, 1 - x, core)
    sib_xn, sib_yn = at(y, 1 - x, 1 - core), at(1 - y, x, 1 - core)
    sib_dg = at(1 - y, 1 - x, 1 - core)

    far = z // 2
    out = 1 - 2 * far
    mid = z * (1 - far) + (3 - z) * far
    ahead, behind = z + out, z - out

    def chunk(p):
        mirrored = (1 - mid) * (3 - p) + mid * (3, 0, 2, 1)[p]
        return mirrored * (1 - far) + (3 - mirrored) * far

    def remote(src, dst, ss, rs, device):
        return pltpu.make_async_remote_copy(
            src_ref=src, dst_ref=dst, send_sem=ss, recv_sem=rs,
            device_id=device, device_id_type=MESH,
        )

    w_copy = pltpu.make_async_copy(w_hbm, w_ref, w_sem)
    w_copy.start()

    barrier = pltpu.get_barrier_semaphore()
    for step in range(1, ctx):
        pl.semaphore_signal(
            barrier, inc=1, device_id=(lax.rem(c + step, ctx), z), device_id_type=MESH
        )
    pl.semaphore_signal(barrier, inc=1, device_id=(c, ahead), device_id_type=MESH)

    @pl.when(mid == 1)
    def _():
        pl.semaphore_signal(barrier, inc=1, device_id=(c, behind), device_id_type=MESH)

    first = pl.multiple_of(z * kv_here * HD, kv_here * HD)
    kv[c, :, : kv_here * HD] = k_ref[:, pl.ds(first, kv_here * HD)]
    kv[c, :, kv_here * HD :] = v_ref[:, pl.ds(first, kv_here * HD)]
    docs[c] = jnp.broadcast_to(drow_ref[...], docs.shape[1:])
    pl.semaphore_wait(barrier, ctx + mid)

    def moves(buf, ss, rs):
        half = buf.shape[1] // 2
        lower, upper = pl.ds(0, half), pl.ds(half, half)
        own = [
            remote(buf.at[c], buf.at[c], ss.at[0], rs.at[0], (sib, z)),
            remote(buf.at[c], buf.at[c], ss.at[1], rs.at[1], (xn, z)),
            remote(buf.at[c], buf.at[c], ss.at[2], rs.at[2], (yn, z)),
        ]
        fwd = [
            remote(buf.at[xn, lower], buf.at[xn, lower], ss.at[3], rs.at[3], (yn, z)),
            remote(buf.at[yn, upper], buf.at[yn, upper], ss.at[4], rs.at[4], (xn, z)),
            remote(buf.at[xn], buf.at[xn], ss.at[5], rs.at[5], (sib, z)),
            remote(buf.at[yn], buf.at[yn], ss.at[6], rs.at[6], (sib, z)),
            remote(buf.at[dg, lower], buf.at[dg, lower], ss.at[7], rs.at[7], (sib, z)),
            remote(buf.at[dg, upper], buf.at[dg, upper], ss.at[8], rs.at[8], (sib, z)),
        ]

        def got(n, view):
            remote(view, view, ss.at[n], rs.at[n], (sib, z)).wait_recv()

        def start_own():
            for copy in own:
                copy.start()

        def forward_near():
            got(1, buf.at[xn])
            fwd[0].start()
            fwd[2].start()
            got(2, buf.at[yn])
            fwd[1].start()
            fwd[3].start()

        def forward_diagonal():
            got(3, buf.at[dg, lower])
            fwd[4].start()
            got(4, buf.at[dg, upper])
            fwd[5].start()

        def all_in():
            got(0, buf.at[sib])
            got(5, buf.at[sib_xn])
            got(6, buf.at[sib_yn])
            got(7, buf.at[sib_dg, lower])
            got(8, buf.at[sib_dg, upper])

        def all_sent():
            for copy in own + fwd:
                copy.wait_send()

        return start_own, forward_near, forward_diagonal, all_in, all_sent

    kv_moves = moves(kv, kv_send, kv_recv)
    kv_moves[0]()
    doc_copies = []
    for step in range(1, ctx):
        peer = lax.rem(c + step, ctx)
        doc_copies.append(
            remote(docs.at[c], docs.at[c], doc_send.at[step], doc_recv.at[step], (peer, z))
        )
        doc_copies[-1].start()
    kv_moves[1]()
    kv_moves[2]()
    for step in range(1, ctx):
        source = lax.rem(c + ctx - step, ctx)
        remote(
            docs.at[source], docs.at[source], doc_send.at[step], doc_recv.at[step], (source, z)
        ).wait_recv()
    kv_moves[3]()

    pair = 2
    keys = pair * tokens
    blocks = c // pair + 1

    def attend(p):
        t = chunk(p)
        begin = pl.multiple_of(t * rows, rows)
        q_pos = c * tokens + t * rows + lax.broadcasted_iota(jnp.int32, (rows, keys), 0)
        q_doc = dcol_ref[pl.ds(begin, rows), :]
        for g in range(kv_here):
            q = jnp.concatenate(
                [
                    q_ref[pl.ds(begin, rows), (g * per_kv + h) * HD : (g * per_kv + h + 1) * HD]
                    for h in range(per_kv)
                ],
                axis=0,
            )

            def body(b, carry):
                old_max, acc = carry
                k = kv[pl.ds(pair * b, pair), :, g * HD : (g + 1) * HD].reshape(keys, HD)
                v = kv[
                    pl.ds(pair * b, pair), :, (kv_here + g) * HD : (kv_here + g + 1) * HD
                ].reshape(keys, HD)
                k_doc = jnp.concatenate(
                    [docs[pair * b + n][0:1, :] for n in range(pair)], axis=1
                )
                k_pos = b * keys + lax.broadcasted_iota(jnp.int32, (rows, keys), 1)
                bias = jnp.where((k_pos <= q_pos) & (k_doc == q_doc), 0.0, -1e30).astype(F32)
                s = lax.dot_general(
                    q, k, (((1,), (1,)), ((), ())), preferred_element_type=F32
                ) * SCALE2
                s = (s.reshape(per_kv, rows, keys) + bias[None]).reshape(per_kv * rows, keys)
                new_max = jnp.maximum(old_max, jnp.max(s, axis=1, keepdims=True))
                weights = jnp.exp2(s - new_max).astype(BF16)
                v_ones = jnp.concatenate([v, jnp.ones((keys, HD), BF16)], axis=1)
                acc = acc * jnp.exp2(old_max - new_max) + jnp.dot(
                    weights, v_ones, preferred_element_type=F32
                )
                return new_max, acc

            _, acc = lax.fori_loop(
                0,
                blocks,
                body,
                (
                    jnp.full((per_kv * rows, 1), -1e30, F32),
                    jnp.zeros((per_kv * rows, 2 * HD), F32),
                ),
            )
            o = (acc[:, :HD] / acc[:, HD:]).astype(BF16)
            for h in range(per_kv):
                att[p, c, :, (g * per_kv + h) * HD : (g * per_kv + h + 1) * HD] = o[
                    h * rows : (h + 1) * rows
                ]

    def project(p):
        def body(j, _):
            a = att[p].reshape(ctx * rows, att.shape[3])
            w = w_ref[:, pl.ds(pl.multiple_of(j * unit, unit), unit)]
            part[p, j] = jnp.dot(a, w, preferred_element_type=F32).astype(BF16)
            return 0

        lax.fori_loop(0, UNITS, body, 0)

    def end_hop(p, j):
        return remote(
            part.at[p, j], zin.at[(0, 2, 3)[p], j], z_send.at[p, j],
            z_recv.at[(0, 2, 3)[p], j], (c, ahead),
        )

    def mid_hop(p, j):
        return remote(
            part.at[p, j], zin.at[(1, 0, 4)[p], j], z_send.at[p, j],
            z_recv.at[(1, 0, 4)[p], j], (c, (ahead, behind, ahead)[p]),
        )

    def z_got(slot, j):
        remote(
            zin.at[slot, j], zin.at[slot, j], z_send.at[0, j], z_recv.at[slot, j], (c, ahead)
        ).wait_recv()

    def end_start(p):
        @pl.when(mid == 0)
        def _():
            for j in range(UNITS):
                end_hop(p, j).start()

    def pass_on(*units):
        @pl.when(mid == 1)
        def _():
            for p, j in units:
                z_got(p, j)
                part[p, j] = (part[p, j].astype(F32) + zin[p, j].astype(F32)).astype(BF16)
                mid_hop(p, j).start()

    w_copy.wait()
    steps = [
        moves(att.at[p], att_send.at[p], att_recv.at[p]) for p in range(4)
    ]
    attend(0)
    steps[0][0]()
    attend(1)
    steps[0][1]()
    steps[1][0]()
    steps[0][2]()
    steps[0][3]()
    project(0)
    end_start(0)
    attend(2)
    pass_on((0, 0))
    steps[1][1]()
    steps[2][0]()
    steps[1][2]()
    steps[1][3]()
    project(1)
    end_start(1)
    pass_on((0, 1), (1, 0))
    attend(3)
    steps[2][1]()
    steps[3][0]()
    steps[2][2]()
    steps[2][3]()
    project(2)
    end_start(2)
    pass_on((0, 2), (1, 1), (0, 3), (1, 2))
    steps[3][1]()
    steps[3][2]()
    steps[3][3]()
    project(3)
    pass_on((1, 3), (2, 0), (2, 1), (2, 2), (2, 3))

    x_copies = []
    for j in range(UNITS):
        @pl.when(mid == 0)
        def _():
            z_got(0, j)
            total = part[3, j].astype(F32) + zin[0, j].astype(F32)
            fin[j] = total.astype(BF16).reshape(fin.shape[1:])

        @pl.when(mid == 1)
        def _():
            z_got(4, j)
            z_got(3, j)
            total = part[3, j].astype(F32) + zin[3, j].astype(F32) + zin[4, j].astype(F32)
            fin[j] = total.astype(BF16).reshape(fin.shape[1:])

        columns = pl.ds(pl.multiple_of(c * width + j * unit, unit), unit)
        for step in range(1, ctx):
            peer = lax.rem(c + step, ctx)
            x_copies.append(
                remote(
                    fin.at[j, peer], out_ref.at[:, columns], x_send.at[step, j],
                    x_recv.at[step, j], (peer, z),
                )
            )
            x_copies[-1].start()
        out_ref[:, columns] = fin[j, c]

    for j in range(UNITS):
        for step in range(1, ctx):
            source = lax.rem(c + ctx - step, ctx)
            columns = pl.ds(pl.multiple_of(source * width + j * unit, unit), unit)
            remote(
                fin.at[j, source], out_ref.at[:, columns], x_send.at[step, j],
                x_recv.at[step, j], (source, z),
            ).wait_recv()

    kv_moves[4]()
    for copy in doc_copies + x_copies:
        copy.wait_send()
    for step in steps:
        step[4]()

    @pl.when(mid == 0)
    def _():
        for p in range(3):
            for j in range(UNITS):
                end_hop(p, j).wait_send()

    @pl.when(mid == 1)
    def _():
        for p in range(3):
            for j in range(UNITS):
                mid_hop(p, j).wait_send()


def fused(ctx, tp, queries, key_rows, value_rows, documents, out_weight):
    tokens, heads_width = queries.shape
    kv_here = heads_width // HD // (HEADS // KV_HEADS)
    rows = tokens // tp
    depth, width = out_weight.shape
    unit = width // UNITS
    vmem = pl.BlockSpec(memory_space=pltpu.VMEM)
    dma = pltpu.SemaphoreType.DMA
    return pl.pallas_call(
        fused_kernel,
        out_shape=jax.ShapeDtypeStruct((rows, width * ctx), BF16),
        in_specs=[vmem] * 5 + [pl.BlockSpec(memory_space=pl.ANY)],
        out_specs=vmem,
        scratch_shapes=[
            pltpu.VMEM((depth, width), BF16),
            pltpu.VMEM((ctx, tokens, 2 * kv_here * HD), BF16),
            pltpu.VMEM((ctx, 8, tokens), jnp.int32),
            pltpu.VMEM((tp, ctx, rows, heads_width), BF16),
            pltpu.VMEM((tp, UNITS, ctx * rows, unit), BF16),
            pltpu.VMEM((5, UNITS, ctx * rows, unit), BF16),
            pltpu.VMEM((UNITS, ctx, rows, unit), BF16),
            dma,
            dma((9,)),
            dma((9,)),
            dma((ctx,)),
            dma((ctx,)),
            dma((tp, 9)),
            dma((tp, 9)),
            dma((3, UNITS)),
            dma((5, UNITS)),
            dma((ctx, UNITS)),
            dma((ctx, UNITS)),
        ],
        compiler_params=pltpu.CompilerParams(
            collective_id=0, has_side_effects=True, vmem_limit_bytes=56 * 1024 * 1024
        ),
    )(
        queries, key_rows, value_rows, documents.reshape(tokens, 1),
        documents.reshape(1, tokens), out_weight,
    )


def general(ctx, tp, queries, key_rows, value_rows, documents, out_weight):
    tokens = queries.shape[0]
    heads_here = queries.shape[1] // HD
    group_size = HEADS // KV_HEADS
    kv_here = max(1, heads_here // group_size)
    per_kv = heads_here // kv_here
    kv_first = lax.axis_index("tp") * heads_here // group_size
    own_keys = lax.dynamic_slice_in_dim(key_rows, kv_first * HD, kv_here * HD, 1)
    own_values = lax.dynamic_slice_in_dim(value_rows, kv_first * HD, kv_here * HD, 1)
    q = queries.reshape(tokens, kv_here, per_kv, HD)
    keys = lax.all_gather(own_keys, "ctx", axis=0, tiled=True).reshape(-1, kv_here, HD)
    values = lax.all_gather(own_values, "ctx", axis=0, tiled=True).reshape(-1, kv_here, HD)
    docs = lax.all_gather(documents, "ctx", axis=0, tiled=True)
    q_pos = lax.axis_index("ctx") * tokens + jnp.arange(tokens, dtype=jnp.int32)
    k_pos = jnp.arange(keys.shape[0], dtype=jnp.int32)
    allowed = (k_pos[None, :] <= q_pos[:, None]) & (docs[None, :] == documents[:, None])
    scores = jnp.einsum("tghd,ngd->ghtn", q, keys, preferred_element_type=F32) / math.sqrt(HD)
    row_max = jnp.max(jnp.where(allowed, scores, -1e30), axis=3, keepdims=True)
    weights = jnp.where(allowed, jnp.exp(scores - row_max), 0.0)
    total = jnp.transpose(jnp.sum(weights, axis=3), (2, 0, 1))[..., None]
    mixed = jnp.einsum("ghtn,ngd->tghd", weights.astype(BF16), values, preferred_element_type=F32)
    attended = (mixed / total).astype(BF16).reshape(tokens, heads_here * HD)
    gathered = lax.all_gather(attended, "ctx", axis=0, tiled=True)
    terms = jnp.dot(gathered, out_weight, preferred_element_type=F32).astype(BF16)
    terms = jnp.transpose(terms.reshape(ctx, tp, tokens // tp, -1), (1, 0, 2, 3))
    summed = lax.psum_scatter(terms, "tp", scatter_dimension=0, tiled=True)[0]
    return lax.all_to_all(summed, "ctx", split_axis=0, concat_axis=2, tiled=True)[0]


def solution(mesh):
    ctx, tp = mesh.shape["ctx"], mesh.shape["tp"]
    on_device = functools.partial(fused if (ctx, tp) == (8, 4) else general, ctx, tp)
    in_specs = (P("ctx", "tp"), P("ctx", None), P("ctx", None), P("ctx"), P("tp", "ctx"))
    return jax.shard_map(
        on_device, mesh=mesh, in_specs=in_specs,
        out_specs=P(("ctx", "tp"), None), check_vma=False,
    )
```

time: 324 us -> 126 us (0.39)
  waiting for transfers between devices: 221 us -> 0 us
  Pallas kernels: 0 us -> 120 us
  matrix products: 51.7 us -> 0 us
  other arithmetic: 16.8 us -> 0 us
  between operations: 13.8 us -> 0.01 us
  blocking collectives: 9.52 us -> 0 us
  local copies, waits for them, and re-layouts: 9.73 us -> 3.73 us
    all_gather x3 -> x0, waiting for transfers between devices: 143 us -> none  [the longest x1 105 us: on_device(): lax.all_gather(out_weight, 'ctx', axis=1, tiled=True)]
    pallas_call x0 -> x1, Pallas kernels: none -> 120 us  [fused(): pl.pallas_call(fused_kernel, out_shape=jax.ShapeDtypeStruct((rows, width...]
    reduce_scatter x1 -> x0, waiting for transfers between devices: 76.6 us -> none  [on_device(): lax.psum_scatter(terms.astype(jnp.bfloat16), 'tp', scatter_dimension=0, t...]
    dot_general x3 -> x0, matrix products: 51.7 us -> none  [the longest x1 18.2 us: update(): jnp.einsum('tghd,ngd->ghtn', query_block, key_block, preferred_element_ty...]
    reduce_sum x1 -> x0, other arithmetic: 14.4 us -> none  [update(): new_sum = jnp.sum(weights, axis=3)]
    all_gather x1 -> x0, blocking collectives: 9.52 us -> none  [on_device(): lax.all_gather(documents, 'ctx', axis=0, tiled=True)]
    cond x4 -> x0, local copies, waits for them, and re-layouts: 3.37 us -> none  [the longest x1 1.92 us: absorb_group(): return lax.cond(start <= query_pos[-1], update, lambda inner: inner, state)]
  transfers between devices with their start and end apart: 4 -> 0, of which waited for: 4 -> 0; matrix products, arithmetic and copies ran while one was open for 19% -> 0% of each run, Pallas kernels for 0% -> 0%
where the time goes in v1:
time: 126 us; the launch traced here: 124 us
  Pallas kernels  120 us (95%)
  local copies, waits for them, and re-layouts  3.73 us (3%)
    pallas_call x1, Pallas kernels, fused(): pl.pallas_call(fused_kernel, out_shape=jax.ShapeDtypeStruct((rows, width...  120 us

profile of v1, /device:TPU:9, one launch (start us, length us, event | category | flops | bytes accessed | tf_op | source)
XLA Modules:
  0.0 123.9 jit_solution(4354986166808923443)
XLA Ops:
  0.0 1.5 %copy.6.dcol_ref = s32[256,1]{1,0:T(8,128)} copy(s32[256,1]{0,1:T(1,128)} %bitcast.2) | data formatting | bytes 2048 | tf_op jit(solution)/shard_map/reshape | solution.py:375
  1.5 120.2 %shard_map.55 = bf16[64,8192]{1,0:T(8,128)(2,1)} custom-call(bf16[256,2048]{1,0:T(8,128)(2,1)} %q_ref.1, bf16[256,1024]{1,0:T(8,128)(2,1)} %k_ref.1, bf16[256,1024]{1,0:T(8,128)(2,1)} %v_ref.1, s32[256,1]{1,0:T(8,128)} %copy.6.dcol_ref, s32[1,256]{1,0:T(1,128)} %bitcast.3, bf16[2048,1024]{1,0:T(8,128)(2,1)} %w_hbm.1), custom_call_target="tpu_custom_call" | custom-call | tf_op jit(solution)/shard_map/pallas_call | solution.py:346
  121.6 2.3 %copy.8 = bf16[64,8192]{1,0:T(8,128)(2,1)} copy(bf16[64,8192]{1,0:T(8,128)(2,1)} %shard_map.55) | data formatting | bytes 2097152
